TPU v7x, 32 devices: a whole 2x2x4 slice. The times are simulated.
32 devices in a mesh: parts: 2 (over x), fsdp: 8 (over z, y), dp: 2 (over core).
Axes of the slice: x: 2, y: 2, z: 4, core: 2. Of those that a mesh axis runs over, the one named last changes fastest.
Arguments:
- tokens: bfloat16 [64, 256, 2048], P(('parts', 'fsdp', 'dp')), parts along dimension 0, may hold values from -6 to 6
- key_shift: bfloat16 [64, 8, 256], P(('parts', 'fsdp', 'dp')), parts along dimension 0, may hold values from -6 to 258
- counts: int32 [64], P('parts'), parts along dimension 0, may hold values from 1 to 32, as said below
- repack_order: int32 [16, 4], P(('parts', 'fsdp')), parts along dimension 0, may hold values from 0 to 3, each once within a row
- norm_gain: float32 [2048], replicated, may hold values from 0.5 to 1.5
- query_weight: bfloat16 [2048, 1024], P('fsdp'), may hold values from -0.125 to 0.125
- key_weight: bfloat16 [2048, 1024], P('fsdp'), may hold values from -0.125 to 0.125
- value_weight: bfloat16 [2048, 1024], P('fsdp'), may hold values from -0.125 to 0.125
- out_weight: bfloat16 [1024, 2048], P('fsdp'), may hold values from -0.1875 to 0.1875
- cotangent: bfloat16 [64, 256, 2048], P(('parts', 'fsdp', 'dp')), parts along dimension 0, may hold values from -6 to 6
Outputs:
- mixed: bfloat16 [64, 256, 2048], P(('parts', 'fsdp', 'dp')), parts along dimension 0
- grad_out: float32 [2048, 2048], P(('parts', 'fsdp', 'dp')), parts along dimension 0
There are 2 independent parts, one for each index of `parts`. A program takes and returns all parts, laid end to end along the dimension named above; an argument that names none is the same for every part. Nothing has to cross between parts.
Inputs may be any that keep to these rules, and one draw needn't show every extreme that they name: `counts`: agents of each scene; some scene has exactly 32 agents and some exactly one. `repack_order`: each row is a permutation of 0 to 3.
All inputs are finite; a program needn't handle non-finite values.
Results may differ from a plain program's by a relative error of at most 0.0077.
Values may be sent and summed in bfloat16 or wider, within the bound.
A program may use at most 128 MiB of HBM per device.

v0:
```python
import math

import jax
import jax.numpy as jnp
from jax import lax
from jax.sharding import PartitionSpec as P

TSTEP = 8


def attend(queries, key_rows, values, key_shift, live_counts):
    scene_count, slot_rows, proj_width = queries.shape
    head_count = key_shift.shape[1]
    head_dim = proj_width // head_count
    split_shape = (scene_count, slot_rows, head_count, head_dim)
    query_heads = queries.reshape(split_shape)
    key_heads = key_rows.reshape(split_shape)
    value_heads = values.reshape(split_shape)
    scores = jnp.einsum(
        "bqhe,bkhe->bhqk", query_heads, key_heads, preferred_element_type=jnp.float32
    ) * (1.0 / math.sqrt(head_dim))
    scores = scores + key_shift.astype(jnp.float32)[:, :, None, :]
    position = jnp.arange(slot_rows, dtype=jnp.int32)
    moment = position % TSTEP
    agent_index = position // TSTEP
    causal = (moment[None, :] <= moment[:, None])[None, None, :, :]
    present = (agent_index[None, :] < live_counts[:, None])[:, None, None, :]
    scores = jnp.where(causal & present, scores, -1e30)
    row_max = jnp.max(scores, axis=-1, keepdims=True)
    weights = jnp.exp(scores - row_max)
    probabilities = (weights / jnp.sum(weights, axis=-1, keepdims=True)).astype(jnp.bfloat16)
    attended = jnp.einsum(
        "bhqk,bkhe->bqhe", probabilities, value_heads, preferred_element_type=jnp.float32
    )
    return attended.reshape(scene_count, slot_rows, proj_width).astype(jnp.bfloat16)


def body(
    tokens,
    key_shift,
    counts,
    repack_order,
    norm_gain,
    query_weight,
    key_weight,
    value_weight,
    out_weight,
    cotangent,
):
    local_scenes, slot_rows, model_width = tokens.shape
    proj_width = query_weight.shape[1]
    tok_rows = local_scenes * slot_rows
    core_index = lax.axis_index("dp")
    pair_index = lax.axis_index("fsdp")
    group_size = local_scenes * lax.axis_size("dp")
    held_tokens, held_shift = (
        lax.all_gather(tokens, "dp", axis=0, tiled=True),
        lax.all_gather(key_shift, "dp", axis=0, tiled=True),
    )
    chosen = lax.dynamic_slice_in_dim(repack_order[0], core_index * local_scenes, local_scenes)
    packed = held_tokens[chosen]
    shifts = held_shift[chosen]
    live_counts = counts[pair_index * group_size + chosen]
    floats = packed.astype(jnp.float32).reshape(tok_rows, model_width)
    normed = (
        floats * lax.rsqrt(jnp.mean(floats * floats, axis=-1, keepdims=True) + 1e-05) * norm_gain
    ).astype(jnp.bfloat16)
    columns = normed
    query_acc = jnp.dot(
        columns,
        lax.all_gather(query_weight, "fsdp", axis=0, tiled=True),
        preferred_element_type=jnp.float32,
    )
    key_acc = jnp.dot(
        columns,
        lax.all_gather(key_weight, "fsdp", axis=0, tiled=True),
        preferred_element_type=jnp.float32,
    )
    value_acc = jnp.dot(
        columns,
        lax.all_gather(value_weight, "fsdp", axis=0, tiled=True),
        preferred_element_type=jnp.float32,
    )
    split_rows = (local_scenes, slot_rows, proj_width)
    queries = query_acc.astype(jnp.bfloat16).reshape(split_rows)
    key_rows = key_acc.astype(jnp.bfloat16).reshape(split_rows)
    values = value_acc.astype(jnp.bfloat16).reshape(split_rows)
    attended = attend(queries, key_rows, values, shifts, live_counts)
    attended_flat = attended.reshape(tok_rows, proj_width)
    columns = attended_flat
    branch = jnp.dot(
        columns,
        lax.all_gather(out_weight, "fsdp", axis=0, tiled=True),
        preferred_element_type=jnp.float32,
    )
    mixed = (floats + branch).astype(jnp.bfloat16).reshape(local_scenes, slot_rows, model_width)
    cot_flat = cotangent.reshape(tok_rows, model_width)
    fsdp_count = lax.axis_size("fsdp")
    dp_count = lax.axis_size("dp")
    grad_scale = 1.0 / math.sqrt(tok_rows * fsdp_count * dp_count)
    columns = attended_flat
    summed = lax.psum_scatter(
        lax.dot_general(
            columns, cot_flat, (((0,), (0,)), ((), ())), preferred_element_type=jnp.float32
        ),
        ("fsdp", "dp"),
        scatter_dimension=0,
        tiled=True,
    )
    return (mixed, summed * grad_scale)


def solution(mesh):
    return jax.shard_map(
        body,
        mesh=mesh,
        in_specs=(
            P(("parts", "fsdp", "dp"), None, None),
            P(("parts", "fsdp", "dp"), None, None),
            P("parts"),
            P(("parts", "fsdp"), None),
            P(),
            P("fsdp", None),
            P("fsdp", None),
            P("fsdp", None),
            P("fsdp", None),
            P(("parts", "fsdp", "dp"), None, None),
        ),
        out_specs=(P(("parts", "fsdp", "dp"), None, None), P(("parts", "fsdp", "dp"), None)),
        check_vma=False,
    )
```

profile of v0, /device:TPU:0, one launch (start us, length us, event | category | flops | bytes accessed | tf_op | source)
XLA Modules:
  0.0 439.4 jit_solution(15888963297104284819)
XLA Ops:
  7.3 0.7 all-gather.6.cloned.1.call-update
  8.0 0.7 all-gather.10.cloned.1.call-update
  8.7 0.7 all-gather.12.cloned.1.call-update
  9.5 0.5 all-gather.8.cloned.1.call-update
  10.1 0.5 all-gather.14.cloned.1.call-update
  10.7 1.9 all_gather.22
  12.7 0.5 gather_fusion.2
  13.3 0.6 gather_fusion.1
  14.0 0.1 broadcast_compare_fusion
  14.1 0.1 broadcast_and_fusion
  14.3 11.7 %all-gather.6.cloned.1.call-done = bf16[4,256,2048]{2,1,0:T(8,128)(2,1)} async-done(((bf16[2,256,2048]{2,1,0:T(8,128)(2,1)}), bf16[4,256,2048]{2,1,0:T(8,128)(2,1)}) %all-gather.6.cloned.1.call-update) | async-done | bytes 4194320 | tf_op jit(solution)/shard_map/all_gather | solution.py:57
  26.0 4.2 gather_fusion
  30.2 2.1 fusion.1
  32.3 3.5 fusion.3
  35.8 67.0 %all-gather.10.cloned.1.call-done = bf16[2048,1024]{1,0:T(8,128)(2,1)} async-done(((bf16[256,1024]{1,0:T(8,128)(2,1)}), bf16[2048,1024]{1,0:T(8,128)(2,1)}) %all-gather.10.cloned.1.call-update) | async-done | bytes 4194320 | tf_op jit(solution)/shard_map/all_gather | solution.py:71
  102.7 5.2 %fusion.13 = bf16[64,8,8,128]{3,1,2,0:T(8,128)(2,1)S(1)} fusion(bf16[512,2048]{1,0:T(8,128)(2,1)} %fusion.3, bf16[2048,1024]{1,0:T(8,128)(2,1)} %all-gather.10.cloned.1.call-done), kind=kOutput, calls=%fused_computation.26 | convolution fusion | flops 2148007936 | bytes 7340032 | tf_op jit(solution)/shard_map/dot_general | solution.py:69
  107.9 0.3 copy.29
  108.2 68.4 %all-gather.12.cloned.1.call-done = bf16[2048,1024]{1,0:T(8,128)(2,1)} async-done(((bf16[256,1024]{1,0:T(8,128)(2,1)}), bf16[2048,1024]{1,0:T(8,128)(2,1)}) %all-gather.12.cloned.1.call-update) | async-done | bytes 4194320 | tf_op jit(solution)/shard_map/all_gather | solution.py:76
  176.5 5.2 %fusion.14 = bf16[64,8,8,128]{3,1,2,0:T(8,128)(2,1)S(1)} fusion(bf16[512,2048]{1,0:T(8,128)(2,1)} %fusion.3, bf16[2048,1024]{1,0:T(8,128)(2,1)} %all-gather.12.cloned.1.call-done), kind=kOutput, calls=%fused_computation.27 | convolution fusion | flops 2148007936 | bytes 7340032 | tf_op jit(solution)/shard_map/dot_general | solution.py:74
  181.7 1.3 copy.30
  183.0 67.3 %all-gather.8.cloned.1.call-done = bf16[2048,1024]{1,0:T(8,128)(2,1)} async-done(((bf16[256,1024]{1,0:T(8,128)(2,1)}), bf16[2048,1024]{1,0:T(8,128)(2,1)}) %all-gather.8.cloned.1.call-update) | async-done | bytes 4194320 | tf_op jit(solution)/shard_map/all_gather | solution.py:81
  250.2 5.2 %fusion.12 = bf16[64,8,8,128]{3,1,2,0:T(8,128)(2,1)S(1)} fusion(bf16[512,2048]{1,0:T(8,128)(2,1)} %fusion.3, bf16[2048,1024]{1,0:T(8,128)(2,1)} %all-gather.8.cloned.1.call-done), kind=kOutput, calls=%fused_computation.25 | convolution fusion | flops 2148007936 | bytes 7340032 | tf_op jit(solution)/shard_map/dot_general | solution.py:79
  255.5 0.3 copy.28
  255.8 0.7 fusion.18
  256.5 2.5 fusion.26
  259.0 0.6 fusion.11
  259.7 5.6 %convolution_bitcast_fusion = f32[1024,2048]{1,0:T(8,128)} fusion(bf16[2,256,1024]{1,2,0:T(8,128)(2,1)S(1)} %bitcast.55, bf16[2,256,2048]{2,1,0:T(8,128)(2,1)S(1)} %copy-done), kind=kOutput, calls=%fused_computation.4 | convolution fusion | flops 2147483648 | bytes 11534336 | tf_op jit(solution)/shard_map/dot_general | solution.py:103
  265.2 1.5 copy.25
  266.7 57.2 %all-gather.14.cloned.1.call-done = bf16[1024,2048]{1,0:T(8,128)(2,1)} async-done(((bf16[128,2048]{1,0:T(8,128)(2,1)}), bf16[1024,2048]{1,0:T(8,128)(2,1)}) %all-gather.14.cloned.1.call-update) | async-done | bytes 4194320 | tf_op jit(solution)/shard_map/all_gather | solution.py:93
  323.9 6.8 %fusion.4 = bf16[512,2048]{1,0:T(8,128)(2,1)} fusion(bf16[2,256,2048]{2,1,0:T(8,128)(2,1)} %gather_fusion, bf16[1024,2048]{1,0:T(8,128)(2,1)} %all-gather.14.cloned.1.call-done, bf16[64,8,8,128]{3,2,1,0:T(8,128)(2,1)} %bitcast.58), kind=kOutput, calls=%fused_computation.11 | convolution fusion | flops 2150629376 | bytes 9437184 | tf_op jit(solution)/shard_map/dot_general | solution.py:91
  330.7 100.0 %reduce-scatter.2.cloned.1.call-done = f32[64,2048]{1,0:T(8,128)} async-done(((f32[1024,2048]{1,0:T(8,128)}), f32[64,2048]{1,0:T(8,128)}) %reduce-scatter.2.cloned.1.call-update) | async-done | bytes 524304 | tf_op jit(solution)/shard_map/reduce_scatter | solution.py:102
  430.7 1.9 broadcast_multiply_fusion
  (28 shorter events, 0.5 us)
Async XLA Ops:
  7.2 252.5 %copy-start = (bf16[2,256,2048]{2,1,0:T(8,128)(2,1)S(1)}, bf16[2,256,2048]{2,1,0:T(8,128)(2,1)}, u32[]{:S(2)}) copy-start(bf16[2,256,2048]{2,1,0:T(8,128)(2,1)} %param.19) | copy-start | bytes 6291460
  7.2 3.5 copy-start.4
  7.2 5.4 %copy-start.5 = (s32[1,4]{1,0:T(1,128)S(1)}, s32[1,4]{1,0:T(1,128)}, u32[]{:S(2)}) copy-start(s32[1,4]{1,0:T(1,128)} %param.13) | copy-start | bytes 52
  7.2 6.1 %copy-start.1 = (s32[32]{0:T(128)S(1)}, s32[32]{0:T(128)}, u32[]{:S(2)}) copy-start(s32[32]{0:T(128)} %param.12) | copy-start | bytes 388
  7.2 18.8 %all-gather.6.cloned.1.call-start = ((), (), s32[]{:S(2)}) async-start(), calls=%async_computation.1 | async-start | bytes 6291456 | tf_op jit(solution)/shard_map/all_gather | solution.py:57
  7.9 94.8 %all-gather.10.cloned.1.call-start = ((), (), s32[]{:S(2)}) async-start(), calls=%async_computation.3 | async-start | bytes 4718592 | tf_op jit(solution)/shard_map/all_gather | solution.py:71
  8.7 167.9 %all-gather.12.cloned.1.call-start = ((), (), s32[]{:S(2)}) async-start(), calls=%async_computation.4 | async-start | bytes 4718592 | tf_op jit(solution)/shard_map/all_gather | solution.py:76
  9.4 22.9 %copy-start.3 = (f32[2048]{0:T(1024)S(1)}, f32[2048]{0:T(1024)}, u32[]{:S(2)}) copy-start(f32[2048]{0:T(1024)} %param.14) | copy-start | bytes 24580
  9.4 240.8 %all-gather.8.cloned.1.call-start = ((), (), s32[]{:S(2)}) async-start(), calls=%async_computation.2 | async-start | bytes 4718592 | tf_op jit(solution)/shard_map/all_gather | solution.py:81
  10.0 313.9 %all-gather.14.cloned.1.call-start = ((), (), s32[]{:S(2)}) async-start(), calls=%async_computation.5 | async-start | bytes 4718592 | tf_op jit(solution)/shard_map/all_gather | solution.py:93
  10.6 420.1 %reduce-scatter.2.cloned.1.call-start = ((), (), s32[]{:S(2)}) async-start(), calls=%async_computation.6 | async-start | bytes 8912896 | tf_op jit(solution)/shard_map/reduce_scatter | solution.py:102
  250.2 5.5 %copy-start.2 = (bf16[64,8,8,128]{3,2,1,0:T(8,128)(2,1)S(1)}, bf16[64,8,8,128]{3,2,1,0:T(8,128)(2,1)}, u32[]{:S(2)}) copy-start(bf16[64,8,8,128]{3,2,1,0:T(8,128)(2,1)} %copy.30) | copy-start | bytes 3145732
Sparse Core Ops, SparseCore 0:
  9.6 16.3 all-gather.5
  28.1 74.5 all-gather.9
  104.9 71.6 all-gather.11
  178.5 71.6 all-gather.7
  252.2 71.6 all-gather.13
  327.8 102.8 reduce-scatter.1
where the time goes:
time: 440 us; the launch traced here: 439 us
  waiting for transfers between devices  375 us (85%)
  matrix products  29.3 us (7%)
  between operations  14.3 us (3%)
  other arithmetic  10.4 us (2%)
  local copies, waits for them, and re-layouts  8.7 us (2%)
    reduce_scatter x1, waiting for transfers between devices, body(): lax.psum_scatter(lax.dot_general(columns, cot_flat, (((0,), (0,)), ((), (...  100 us
    all_gather x1, waiting for transfers between devices, body(): lax.all_gather(key_weight, 'fsdp', axis=0, tiled=True)  68.4 us
    all_gather x1, waiting for transfers between devices, body(): lax.all_gather(value_weight, 'fsdp', axis=0, tiled=True)  67.3 us
    all_gather x1, waiting for transfers between devices, body(): lax.all_gather(query_weight, 'fsdp', axis=0, tiled=True)  67 us
    all_gather x1, waiting for transfers between devices, body(): lax.all_gather(out_weight, 'fsdp', axis=0, tiled=True)  57.2 us
    all_gather x1, waiting for transfers between devices, body(): lax.all_gather(tokens, 'dp', axis=0, tiled=True)  11.7 us
  transfers between devices with their start and end apart: 6, of which 6 were waited for; matrix products, arithmetic and copies ran while one was open for 11% of the time, Pallas kernels for 0%

commit v1 on v0

v1 whole, which is shorter than its diff:
```python
import functools
import math

import jax
import jax.numpy as jnp
from jax import lax
from jax.experimental import pallas as pl
from jax.experimental.pallas import tpu as pltpu
from jax.sharding import PartitionSpec as P

TSTEP = 8
WIDE = 512
MESH = pl.DeviceIdType.MESH
BF16, F32 = jnp.bfloat16, jnp.float32


def cut(rows):
    return max(16, rows * 5 // 16 // 16 * 16)


def kernel(
    n, heads,
    order_ref, counts_ref, gain_ref, tok_ref, shift_ref, wq_ref, wk_ref, wv_ref, wo_ref, cot_ref,
    mixed_ref, grad_ref,
    held, heldshift, shf, normed, buf, obuf, acc, att, cot, gmine, gsend, gsib, rrecv, rsend,
    mixs, gout,
    loc_sem, tok_sem, out_sem,
    a_ring, a_sib, a_x, a_sibx,
    b_ring, b_sib, b_x, b_sibx,
    gs_sem, r_sem,
):
    dp, fs, part = lax.axis_index("dp"), lax.axis_index("fsdp"), lax.axis_index("parts")
    rows = normed.shape[2]
    orows = wo_ref.shape[0]
    pa, pb = buf.shape[0] // 2, obuf.shape[0] // 2
    ma, mb = (n - 1) * pa, (n - 1) * pb
    tok_rows = normed.shape[1]
    slot = tok_rows // 2
    hd = att.shape[1] // heads
    rp = gmine.shape[2]
    gp = gmine.shape[1]
    rem, div = lax.rem, lax.div

    half = n // 2
    side = rem(fs, 2)
    r = (1 - side) * div(fs, 2) + side * (n - 1 - div(fs, 2))
    way = 1 - 2 * dp

    def at(q):
        q = rem(q + n, n)
        back = div(q, half)
        return (1 - back) * 2 * q + back * (2 * (n - 1 - q) + 1)

    nxt = {"fsdp": at(r + way)}
    prv = {"fsdp": at(r - way)}
    sib = {"dp": 1 - dp}
    xp = rem(part, 2)
    xdev = {"parts": part + 1 - 2 * xp}

    barrier = pltpu.get_barrier_semaphore()
    for dev in (nxt, prv, sib, xdev):
        pl.semaphore_signal(barrier, inc=1, device_id=dev, device_id_type=MESH)
    pl.semaphore_wait(barrier, 4)

    def rcopy(src, dst, sems, i, dev):
        return pltpu.make_async_remote_copy(
            src_ref=src, dst_ref=dst, send_sem=sems.at[0, i], recv_sem=sems.at[1, i],
            device_id=dev, device_id_type=MESH,
        )

    def part_rows(height):
        a = cut(height)
        ring = (a * xp, height - a)
        mine = ((height - a) * xp, a)
        other = ((height - a) * (1 - xp), a)
        return ring, mine, other

    def piece(ref, p, owner, height, span):
        start = pl.multiple_of(owner * height + span[0], 16)
        return ref.at[p, pl.ds(start, span[1]), :]

    ring_a, mine_a, other_a = part_rows(rows)
    ring_b, mine_b, other_b = part_rows(orows)

    class Gather:
        def __init__(self, ref, height, count, spans, ring, sibl, x, sibx):
            self.ref, self.height, self.count = ref, height, count
            self.ring_rows, self.mine, self.other = spans
            self.ring, self.sibl, self.x, self.sibx = ring, sibl, x, sibx
            self.total = (n - 1) * count

        def here(self, m):
            return at(r - way * (div(m, self.count) + 1)), dp * self.count + rem(m, self.count)

        def there(self, m):
            return at(r + way * (div(m, self.count) + 1)), (1 - dp) * self.count + rem(m, self.count)

        def cp(self, kind, m, where):
            owner, p = where
            span, sems, dev = {
                "ring": (self.ring_rows, self.ring, nxt),
                "sib": (self.ring_rows, self.sibl, sib),
                "x": (self.mine, self.x, xdev),
                "xin": (self.other, self.x, xdev),
                "sibx": (self.other, self.sibx, sib),
            }[kind]
            ref = piece(self.ref, p, owner, self.height, span)
            return rcopy(ref, ref, sems, m, dev)

        def step(self, m):
            w = self.here(m)
            self.cp("ring", m, w).wait_recv()

            @pl.when(m < self.total - self.count)
            def _():
                self.cp("ring", m + self.count, w).start()

            self.cp("x", m, w).start()
            self.cp("sib", m, w).start()

        def step_x(self, m):
            w = self.here(m)
            self.cp("xin", m, w).wait_recv()
            self.cp("sibx", m, w).start()

        def arrived(self, m):
            w = self.there(m)
            self.cp("sib", m, w).wait_recv()
            self.cp("sibx", m, w).wait_recv()

        def drain(self):
            @pl.loop(0, self.total)
            def _(m):
                w = self.here(m)
                self.cp("ring", m, w).wait_send()
                self.cp("x", m, w).wait_send()
                self.cp("sib", m, w).wait_send()
                self.cp("sibx", m, w).wait_send()

    ga = Gather(buf, rows, pa, (ring_a, mine_a, other_a), a_ring, a_sib, a_x, a_sibx)
    gb = Gather(obuf, orows, pb, (ring_b, mine_b, other_b), b_ring, b_sib, b_x, b_sibx)

    def own_cols(j):
        return pl.ds(pl.multiple_of((dp * pb + j) * WIDE, WIDE), WIDE)

    weights = (wq_ref, wk_ref, wv_ref)
    for j in range(pa):
        cols = pl.ds(pl.multiple_of(dp * WIDE, WIDE), WIDE)
        src = weights[j].at[pl.ds(pl.multiple_of(ring_a[0], 16), ring_a[1]), cols]
        dst = piece(buf, dp * pa + j, fs, rows, ring_a)
        rcopy(src, dst, a_ring, j, nxt).start()

    tok_in = held.at[pl.ds(dp * 2, 2)]
    tcopy = rcopy(tok_ref, tok_in, tok_sem, 0, sib)
    tcopy.start()
    scopy = rcopy(shift_ref, heldshift.at[dp], tok_sem, 1, sib)
    scopy.start()

    local = []

    def lcopy(src, dst):
        c = pltpu.make_async_copy(src, dst, loc_sem.at[len(local)])
        c.start()
        local.append(c)

    lcopy(tok_ref, tok_in)
    lcopy(shift_ref, heldshift.at[dp])
    for d in range(2):
        for j in range(pa):
            lcopy(
                weights[j].at[:, pl.ds(d * WIDE, WIDE)],
                piece(buf, d * pa + j, fs, rows, (0, rows)),
            )
    for p in range(2 * pb):
        lcopy(wo_ref.at[:, pl.ds(p * WIDE, WIDE)], piece(obuf, p, fs, orows, (0, orows)))
    lcopy(cot_ref, cot)

    def add(owner, p, first=False):
        start = pl.multiple_of(owner * rows, 16)
        term = jnp.dot(
            normed[owner], buf[p, pl.ds(start, rows), :], preferred_element_type=F32
        )
        if first:
            acc[p] = term
        else:
            acc[p] += term

    def add_here(m):
        add(*ga.here(m))

    def add_there(m):
        ga.arrived(m)
        add(*ga.there(m))

    lead = 2 * pa

    @pl.loop(0, lead)
    def _(m):
        ga.step(m)

        @pl.when(m >= 1)
        def _():
            ga.step_x(m - 1)

    for c in local:
        c.wait()
    rcopy(tok_ref, held.at[pl.ds(2 - dp * 2, 2)], tok_sem, 0, sib).wait_recv()
    rcopy(shift_ref, heldshift.at[1 - dp], tok_sem, 1, sib).wait_recv()
    for d in range(2):
        shf[pl.ds(d * 16, 16), :] = heldshift[d].astype(F32)

    tile = 32
    per = slot // tile

    @pl.loop(0, 2 * per)
    def _(t):
        k = div(t, per)
        chosen = order_ref[0, dp * 2 + k]
        x = held[chosen, pl.ds(pl.multiple_of(rem(t, per) * tile, tile), tile), :].astype(F32)
        scale = lax.rsqrt(jnp.mean(x * x, axis=-1, keepdims=True) + 1e-05)
        y = (x * scale * gain_ref[...]).astype(BF16)
        at_rows = pl.ds(pl.multiple_of(t * tile, tile), tile)
        for c in range(n):
            normed[c, at_rows, :] = y[:, c * rows:(c + 1) * rows]

    @pl.loop(0, 2 * pa)
    def _(p):
        add(fs, p, True)

    @pl.loop(lead, ma + 2)
    def _(m):
        @pl.when(m < ma)
        def _():
            ga.step(m)

        @pl.when(m == ma - pa)
        def _():
            for j in range(pb):
                ref = piece(obuf, dp * pb + j, fs, orows, ring_b)
                rcopy(ref, ref, b_ring, j, nxt).start()

        @pl.when(m <= ma)
        def _():
            ga.step_x(m - 1)
            add_here(m - 1)

        add_there(m - 2)
        late = m - lead

        @pl.when(late < lead - 1)
        def _():
            add_here(late)

        @pl.when(late < lead - 2)
        def _():
            add_there(late)

    per_half = heads // 2
    per_head = hd // (2 * rp)

    def attend(h, k):
        d = div(h, per_half)
        cols = pl.ds(pl.multiple_of(rem(h, per_half) * hd, hd), hd)
        rws = pl.ds(pl.multiple_of(k * slot, slot), slot)
        q = acc[d * 3, rws, cols].astype(BF16)
        kk = acc[d * 3 + 1, rws, cols].astype(BF16)
        v = acc[d * 3 + 2, rws, cols].astype(BF16)
        chosen = order_ref[0, dp * 2 + k]
        live = counts_ref[fs * 4 + chosen]
        row = shf[pl.ds(chosen * 8 + h, 1), :]
        s = lax.dot_general(q, kk, (((1,), (1,)), ((), ())), preferred_element_type=F32)
        s = s * (1.0 / math.sqrt(hd)) + row
        i = lax.broadcasted_iota(jnp.int32, (slot, slot), 0)
        j = lax.broadcasted_iota(jnp.int32, (slot, slot), 1)
        ok = ((j & (TSTEP - 1)) <= (i & (TSTEP - 1))) & (j < live * TSTEP)
        s = jnp.where(ok, s, -1e30)
        w = jnp.exp(s - jnp.max(s, axis=-1, keepdims=True))
        prob = (w * (1.0 / jnp.sum(w, axis=-1, keepdims=True))).astype(BF16)
        o = jnp.dot(prob, v, preferred_element_type=F32).astype(BF16)
        att[rws, pl.ds(pl.multiple_of(h * hd, hd), hd)] = o

    def gcopy(o):
        return rcopy(gsend.at[o], gsib.at[o], gs_sem, o, sib)

    def gradient(h):
        a = att[:, pl.ds(pl.multiple_of(h * hd, hd), hd)]
        for c in range(gp):
            g = lax.dot_general(
                a, cot[:, c * WIDE:(c + 1) * WIDE], (((0,), (0,)), ((), ())),
                preferred_element_type=F32,
            )
            for o in range(per_head):
                g0 = g[(2 * o) * rp:(2 * o + 1) * rp]
                g1 = g[(2 * o + 1) * rp:(2 * o + 2) * rp]
                gmine[h * per_head + o, c] = jnp.where(dp == 0, g0, g1)
                gsend[h * per_head + o, c] = jnp.where(dp == 0, g1, g0).astype(BF16)
        for o in range(per_head):
            gcopy(h * per_head + o).start()

    @pl.loop(0, max(mb + 1, 2 * heads))
    def _(m):
        @pl.when(m < mb)
        def _():
            gb.step(m)

        @pl.when((m >= 1) & (m <= mb))
        def _():
            gb.step_x(m - 1)

        @pl.when(m < 2 * heads)
        def _():
            attend(div(m, 2), rem(m, 2))

        @pl.when((m < 2 * heads) & (rem(m, 2) == 1))
        def _():
            gradient(div(m, 2))

    @pl.loop(0, mb)
    def _(m):
        gb.arrived(m)

    def mixcopy(k, c):
        cols = pl.ds(pl.multiple_of(c * WIDE, WIDE), WIDE)
        return pltpu.make_async_copy(
            mixs.at[k, :, cols], mixed_ref.at[k, :, cols], out_sem.at[k * 2 * pb + c]
        )

    def mix(t):
        k, c = rem(t, 2), div(t, 2)
        rws = pl.ds(pl.multiple_of(k * slot, slot), slot)
        cols = pl.ds(pl.multiple_of(c * WIDE, WIDE), WIDE)
        branch = jnp.dot(att[rws, :], obuf[c], preferred_element_type=F32)
        chosen = order_ref[0, dp * 2 + k]
        mixs[k, :, cols] = (held[chosen, :, cols].astype(F32) + branch).astype(BF16)
        mixcopy(k, c).start()

    def hop(m):
        return rcopy(rsend.at[m], rrecv.at[m], r_sem, m, nxt)

    scale = 1.0 / math.sqrt(tok_rows * n * 2)

    @pl.loop(0, n * gp)
    def _(m):
        s, c = div(m, gp), rem(m, gp)
        owner = at(r - way * (s + 1))

        @pl.when(c == 0)
        def _():
            gcopy(owner).wait_recv()

        @pl.when(s == 0)
        def _():
            rsend[m] = (gmine[owner, c] + gsib[owner, c].astype(F32)).astype(BF16)
            hop(m).start()

        @pl.when((s > 0) & (s < n - 1))
        def _():
            hop(m - gp).wait_recv()
            rsend[m] = (
                gmine[owner, c] + gsib[owner, c].astype(F32) + rrecv[m - gp].astype(F32)
            ).astype(BF16)
            hop(m).start()

        @pl.when(s == n - 1)
        def _():
            hop(m - gp).wait_recv()
            gout[:, pl.ds(pl.multiple_of(c * WIDE, WIDE), WIDE)] = scale * (
                gmine[owner, c] + gsib[owner, c].astype(F32) + rrecv[m - gp].astype(F32)
            )

        @pl.when((c == gp - 1) & (s < 4 * pb))
        def _():
            mix(s)

    gcp = pltpu.make_async_copy(gout, grad_ref, out_sem.at[4 * pb])
    gcp.start()
    for k in range(2):
        for c in range(2 * pb):
            mixcopy(k, c).wait()

    ga.drain()
    gb.drain()
    tcopy.wait_send()
    scopy.wait_send()

    @pl.loop(0, n)
    def _(o):
        gcopy(o).wait_send()

    @pl.loop(0, (n - 1) * gp)
    def _(m):
        hop(m).wait_send()

    gcp.wait()


def body(n, tokens, key_shift, counts, repack_order, norm_gain, wq, wk, wv, wo, cotangent):
    scenes, slot, width = tokens.shape
    rows, proj = wq.shape
    orows = wo.shape[0]
    heads = key_shift.shape[1]
    tok_rows = scenes * slot
    rp = proj // (2 * n)
    gp = width // WIDE
    pa, pb = 3 * proj // 2 // WIDE, width // 2 // WIDE
    ma, mb = (n - 1) * pa, (n - 1) * pb
    dma = pltpu.SemaphoreType.DMA
    any_spec = pl.BlockSpec(memory_space=pl.ANY)
    smem = pl.BlockSpec(memory_space=pltpu.SMEM)
    vmem = pl.BlockSpec(memory_space=pltpu.VMEM)
    mixed, grad = pl.pallas_call(
        functools.partial(kernel, n, heads),
        out_shape=(
            jax.ShapeDtypeStruct((scenes, slot, width), BF16),
            jax.ShapeDtypeStruct((rp, width), F32),
        ),
        in_specs=[smem, smem, vmem] + [any_spec] * 7,
        out_specs=(any_spec, any_spec),
        scratch_shapes=[
            pltpu.VMEM((2 * scenes, slot, width), BF16),
            pltpu.VMEM((2, scenes * heads, slot), BF16),
            pltpu.VMEM((2 * scenes * heads, slot), F32),
            pltpu.VMEM((n, tok_rows, rows), BF16),
            pltpu.VMEM((2 * pa, n * rows, WIDE), BF16),
            pltpu.VMEM((2 * pb, n * orows, WIDE), BF16),
            pltpu.VMEM((2 * pa, tok_rows, WIDE), F32),
            pltpu.VMEM((tok_rows, proj), BF16),
            pltpu.VMEM((tok_rows, width), BF16),
            pltpu.VMEM((n, gp, rp, WIDE), F32),
            pltpu.VMEM((n, gp, rp, WIDE), BF16),
            pltpu.VMEM((n, gp, rp, WIDE), BF16),
            pltpu.VMEM(((n - 1) * gp, rp, WIDE), BF16),
            pltpu.VMEM(((n - 1) * gp, rp, WIDE), BF16),
            pltpu.VMEM((scenes, slot, width), BF16),
            pltpu.VMEM((rp, width), F32),
            dma((3 + 2 * pa + 2 * pb,)),
            dma((2, 2)),
            dma((4 * pb + 1,)),
            dma((2, ma)), dma((2, ma)), dma((2, ma)), dma((2, ma)),
            dma((2, mb)), dma((2, mb)), dma((2, mb)), dma((2, mb)),
            dma((2, n)),
            dma((2, (n - 1) * gp)),
        ],
        compiler_params=pltpu.CompilerParams(
            collective_id=0, has_side_effects=True, vmem_limit_bytes=60 * 1024 * 1024
        ),
    )(
        repack_order, counts, norm_gain.reshape(1, width), tokens,
        key_shift.reshape(scenes * heads, slot), wq, wk, wv, wo, cotangent.reshape(tok_rows, width),
    )
    return mixed, grad


def solution(mesh):
    return jax.shard_map(
        functools.partial(body, mesh.shape["fsdp"]),
        mesh=mesh,
        in_specs=(
            P(("parts", "fsdp", "dp"), None, None),
            P(("parts", "fsdp", "dp"), None, None),
            P("parts"),
            P(("parts", "fsdp"), None),
            P(),
            P("fsdp", None),
            P("fsdp", None),
            P("fsdp", None),
            P("fsdp", None),
            P(("parts", "fsdp", "dp"), None, None),
        ),
        out_specs=(P(("parts", "fsdp", "dp"), None, None), P(("parts", "fsdp", "dp"), None)),
        check_vma=False,
    )
```

time: 440 us -> 129 us (0.29)
  waiting for transfers between devices: 375 us -> 0 us
  Pallas kernels: 0 us -> 124 us
  matrix products: 29.3 us -> 0 us
  between operations: 14.3 us -> 0.65 us
  other arithmetic: 10.4 us -> 0 us
  local copies, waits for them, and re-layouts: 8.7 us -> 4.01 us
    all_gather x5 -> x0, waiting for transfers between devices: 271 us -> none  [the longest x1 68.4 us: body(): lax.all_gather(key_weight, 'fsdp', axis=0, tiled=True)]
    pallas_call x0 -> x1, Pallas kernels: none -> 124 us  [body(): pl.pallas_call(functools.partial(kernel, n, heads), out_shape=(jax.ShapeD...]
    reduce_scatter x1 -> x0, waiting for transfers between devices: 100 us -> none  [body(): lax.psum_scatter(lax.dot_general(columns, cot_flat, (((0,), (0,)), ((), (...]
    dot_general x7 -> x0, matrix products: 29.3 us -> none  [the longest x1 6.84 us: body(): jnp.dot(columns, lax.all_gather(out_weight, 'fsdp', axis=0, tiled=True),...]
    gather x3 -> x0, local copies, waits for them, and re-layouts: 5.39 us -> none  [the longest x1 4.21 us: body(): packed = held_tokens[chosen]]
  transfers between devices with their start and end apart: 6 -> 0, of which waited for: 6 -> 0; matrix products, arithmetic and copies ran while one was open for 11% -> 0% of each run, Pallas kernels for 0% -> 0%
where the time goes in v1:
time: 129 us
  Pallas kernels  124 us (96%)
  local copies, waits for them, and re-layouts  4.01 us (3%)
    pallas_call x1, Pallas kernels, body(): pl.pallas_call(functools.partial(kernel, n, heads), out_shape=(jax.ShapeD...  124 us
    unnamed x4, local copies, waits for them, and re-layouts  4.01 us

profile of v1, /device:TPU:0, one launch (start us, length us, event | category | flops | bytes accessed | tf_op | source)
XLA Modules:
  0.0 128.9 jit_solution(5512124027408522903)
XLA Ops:
  0.6 124.2 %shard_map.113 = (bf16[2,256,2048]{2,1,0:T(8,128)(2,1)}, f32[64,2048]{1,0:T(8,128)}) custom-call(s32[1,4]{1,0:T(1,128)} %order_ref.1, s32[32]{0:T(128)} %counts_ref.1, f32[1,2048]{1,0:T(1,128)} %bitcast.4, bf16[2,256,2048]{2,1,0:T(8,128)(2,1)} %tok_ref.1, bf16[16,256]{1,0:T(8,128)(2,1)} %bitcast.5, bf16[256,1024]{1,0:T(8,128)(2,1)} %wq_ref.1, ...), custom_call_target="tpu_custom_call" | custom-call | tf_op jit(solution)/shard_map/pallas_call | solution.py:411
  124.9 0.0 copy-start
  124.9 3.2 %copy.14 = bf16[2,256,2048]{2,1,0:T(8,128)(2,1)} copy(bf16[2,256,2048]{2,1,0:T(8,128)(2,1)} %get-tuple-element.4) | data formatting | bytes 4194304
  128.1 0.0 copy-done
  128.1 0.8 copy.15
Async XLA Ops:
  124.9 3.2 %copy-start = (f32[64,2048]{1,0:T(8,128)S(1)}, f32[64,2048]{1,0:T(8,128)}, u32[]{:S(2)}) copy-start(f32[64,2048]{1,0:T(8,128)} %get-tuple-element.5) | copy-start | bytes 1572868

commit v2 on v1

--- a/solution.py
+++ b/solution.py
@@ -192,15 +192,15 @@
         ga.arrived(m)
         add(*ga.there(m))
 
-    lead = 2 * pa
+    lead, lag = 2 * pa, pa
 
     @pl.loop(0, lead)
     def _(m):
         ga.step(m)
 
-        @pl.when(m >= 1)
-        def _():
-            ga.step_x(m - 1)
+        @pl.when(m >= lag)
+        def _():
+            ga.step_x(m - lag)
 
     for c in local:
         c.wait()
@@ -227,7 +227,7 @@
     def _(p):
         add(fs, p, True)
 
-    @pl.loop(lead, ma + 2)
+    @pl.loop(lead, ma + lag + 1)
     def _(m):
         @pl.when(m < ma)
         def _():
@@ -239,19 +239,19 @@
                 ref = piece(obuf, dp * pb + j, fs, orows, ring_b)
                 rcopy(ref, ref, b_ring, j, nxt).start()
 
-        @pl.when(m <= ma)
-        def _():
-            ga.step_x(m - 1)
-            add_here(m - 1)
-
-        add_there(m - 2)
+        @pl.when(m < ma + lag)
+        def _():
+            ga.step_x(m - lag)
+            add_here(m - lag)
+
+        add_there(m - lag - 1)
         late = m - lead
 
-        @pl.when(late < lead - 1)
+        @pl.when(late < lead - lag)
         def _():
             add_here(late)
 
-        @pl.when(late < lead - 2)
+        @pl.when(late < lead - lag - 1)
         def _():
             add_there(late)
 
@@ -297,15 +297,15 @@
         for o in range(per_head):
             gcopy(h * per_head + o).start()
 
-    @pl.loop(0, max(mb + 1, 2 * heads))
+    @pl.loop(0, max(mb + lag, 2 * heads))
     def _(m):
         @pl.when(m < mb)
         def _():
             gb.step(m)
 
-        @pl.when((m >= 1) & (m <= mb))
-        def _():
-            gb.step_x(m - 1)
+        @pl.when((m >= lag) & (m < mb + lag))
+        def _():
+            gb.step_x(m - lag)
 
         @pl.when(m < 2 * heads)
         def _():

time: 129 us -> 114 us (0.88)
  Pallas kernels: 124 us -> 109 us
    pallas_call x1, Pallas kernels: 124 us -> 109 us  [body(): pl.pallas_call(functools.partial(kernel, n, heads), out_shape=(jax.ShapeD...]
where the time goes in v2:
time: 114 us
  Pallas kernels  109 us (96%)
  local copies, waits for them, and re-layouts  4.01 us (4%)
    pallas_call x1, Pallas kernels, body(): pl.pallas_call(functools.partial(kernel, n, heads), out_shape=(jax.ShapeD...  109 us
    unnamed x4, local copies, waits for them, and re-layouts  4.01 us

profile of v2, /device:TPU:0, one launch (start us, length us, event | category | flops | bytes accessed | tf_op | source)
XLA Modules:
  0.0 114.0 jit_solution(10123708317769024066)
XLA Ops:
  0.6 109.3 %shard_map.113 = (bf16[2,256,2048]{2,1,0:T(8,128)(2,1)}, f32[64,2048]{1,0:T(8,128)}) custom-call(s32[1,4]{1,0:T(1,128)} %order_ref.1, s32[32]{0:T(128)} %counts_ref.1, f32[1,2048]{1,0:T(1,128)} %bitcast.4, bf16[2,256,2048]{2,1,0:T(8,128)(2,1)} %tok_ref.1, bf16[16,256]{1,0:T(8,128)(2,1)} %bitcast.5, bf16[256,1024]{1,0:T(8,128)(2,1)} %wq_ref.1, ...), custom_call_target="tpu_custom_call" | custom-call | tf_op jit(solution)/shard_map/pallas_call | solution.py:411
  110.0 0.0 copy-start
  110.0 3.2 %copy.14 = bf16[2,256,2048]{2,1,0:T(8,128)(2,1)} copy(bf16[2,256,2048]{2,1,0:T(8,128)(2,1)} %get-tuple-element.4) | data formatting | bytes 4194304
  113.2 0.0 copy-done
  113.2 0.8 copy.15
Async XLA Ops:
  110.0 3.2 %copy-start = (f32[64,2048]{1,0:T(8,128)S(1)}, f32[64,2048]{1,0:T(8,128)}, u32[]{:S(2)}) copy-start(f32[64,2048]{1,0:T(8,128)} %get-tuple-element.5) | copy-start | bytes 1572868

commit v3 on v2

--- a/solution.py
+++ b/solution.py
@@ -193,6 +193,18 @@
         add(*ga.there(m))
 
     lead, lag = 2 * pa, pa
+    join = 3 * pa
+    early = pb * (n - 4)
+
+    def tick(b):
+        @pl.when(b < mb)
+        def _():
+            gb.step(b)
+
+        @pl.when((b >= lag) & (b < mb + lag))
+        def _():
+            gb.step_x(b - lag)
+
 
     @pl.loop(0, lead)
     def _(m):
@@ -233,11 +245,17 @@
         def _():
             ga.step(m)
 
-        @pl.when(m == ma - pa)
+        @pl.when(m == join - pa)
         def _():
             for j in range(pb):
                 ref = piece(obuf, dp * pb + j, fs, orows, ring_b)
                 rcopy(ref, ref, b_ring, j, nxt).start()
+
+        over = m - join
+
+        @pl.when((over >= 0) & (m < ma) & (rem(over, pa) < pb))
+        def _():
+            tick(div(over, pa) * pb + rem(over, pa))
 
         @pl.when(m < ma + lag)
         def _():
@@ -297,28 +315,6 @@
         for o in range(per_head):
             gcopy(h * per_head + o).start()
 
-    @pl.loop(0, max(mb + lag, 2 * heads))
-    def _(m):
-        @pl.when(m < mb)
-        def _():
-            gb.step(m)
-
-        @pl.when((m >= lag) & (m < mb + lag))
-        def _():
-            gb.step_x(m - lag)
-
-        @pl.when(m < 2 * heads)
-        def _():
-            attend(div(m, 2), rem(m, 2))
-
-        @pl.when((m < 2 * heads) & (rem(m, 2) == 1))
-        def _():
-            gradient(div(m, 2))
-
-    @pl.loop(0, mb)
-    def _(m):
-        gb.arrived(m)
-
     def mixcopy(k, c):
         cols = pl.ds(pl.multiple_of(c * WIDE, WIDE), WIDE)
         return pltpu.make_async_copy(
@@ -339,8 +335,7 @@
 
     scale = 1.0 / math.sqrt(tok_rows * n * 2)
 
-    @pl.loop(0, n * gp)
-    def _(m):
+    def reduce_step(m):
         s, c = div(m, gp), rem(m, gp)
         owner = at(r - way * (s + 1))
 
@@ -368,9 +363,45 @@
                 gmine[owner, c] + gsib[owner, c].astype(F32) + rrecv[m - gp].astype(F32)
             )
 
-        @pl.when((c == gp - 1) & (s < 4 * pb))
-        def _():
-            mix(s)
+    units = 2 * heads
+    matched = n == heads
+    ahead = 6
+    begun = units - ahead if matched else 0
+
+    def head_at(i):
+        if not matched:
+            return i
+        return at(r + (2 * rem(i, 2) - 1) * (div(i, 2) + 1) - div(i, n - 1) * (n // 2))
+
+    @pl.loop(0, max(mb - early + lag, units))
+    def _(u):
+        tick(early + u)
+
+        if matched:
+            @pl.when((u >= ahead) & (u < units))
+            def _():
+                reduce_step(u - ahead)
+
+        @pl.when(u < units)
+        def _():
+            attend(head_at(div(u, 2)), rem(u, 2))
+
+        @pl.when((u < units) & (rem(u, 2) == 1))
+        def _():
+            gradient(head_at(div(u, 2)))
+
+    @pl.loop(0, mb)
+    def _(m):
+        gb.arrived(m)
+
+    @pl.loop(begun, n * gp)
+    def _(m):
+        reduce_step(m)
+        past = m - begun
+
+        @pl.when((rem(past, 2) == 0) & (past < 8 * pb))
+        def _():
+            mix(div(past, 2))
 
     gcp = pltpu.make_async_copy(gout, grad_ref, out_sem.at[4 * pb])
     gcp.start()

time: 114 us -> 107 us (0.939)
  Pallas kernels: 109 us -> 102 us
    pallas_call x1, Pallas kernels: 109 us -> 102 us  [body(): pl.pallas_call(functools.partial(kernel, n, heads), out_shape=(jax.ShapeD...]
where the time goes in v3:
time: 107 us
  Pallas kernels  102 us (95%)
  local copies, waits for them, and re-layouts  4.01 us (4%)
    pallas_call x1, Pallas kernels, body(): pl.pallas_call(functools.partial(kernel, n, heads), out_shape=(jax.ShapeD...  102 us
    unnamed x4, local copies, waits for them, and re-layouts  4.01 us

profile of v3, /device:TPU:0, one launch (start us, length us, event | category | flops | bytes accessed | tf_op | source)
XLA Modules:
  0.0 106.8 jit_solution(4361441130502514002)
XLA Ops:
  0.6 102.1 %shard_map.113 = (bf16[2,256,2048]{2,1,0:T(8,128)(2,1)}, f32[64,2048]{1,0:T(8,128)}) custom-call(s32[1,4]{1,0:T(1,128)} %order_ref.1, s32[32]{0:T(128)} %counts_ref.1, f32[1,2048]{1,0:T(1,128)} %bitcast.4, bf16[2,256,2048]{2,1,0:T(8,128)(2,1)} %tok_ref.1, bf16[16,256]{1,0:T(8,128)(2,1)} %bitcast.5, bf16[256,1024]{1,0:T(8,128)(2,1)} %wq_ref.1, ...), custom_call_target="tpu_custom_call" | custom-call | tf_op jit(solution)/shard_map/pallas_call | solution.py:442
  102.7 0.0 copy-start
  102.8 3.2 %copy.14 = bf16[2,256,2048]{2,1,0:T(8,128)(2,1)} copy(bf16[2,256,2048]{2,1,0:T(8,128)(2,1)} %get-tuple-element.4) | data formatting | bytes 4194304
  106.0 0.0 copy-done
  106.0 0.8 copy.15
Async XLA Ops:
  102.7 3.2 %copy-start = (f32[64,2048]{1,0:T(8,128)S(1)}, f32[64,2048]{1,0:T(8,128)}, u32[]{:S(2)}) copy-start(f32[64,2048]{1,0:T(8,128)} %get-tuple-element.5) | copy-start | bytes 1572868

commit v4 on v3

--- a/solution.py
+++ b/solution.py
@@ -15,7 +15,7 @@
 
 
 def cut(rows):
-    return max(16, rows * 5 // 16 // 16 * 16)
+    return max(16, (rows * 5 + 128) // 16 // 16 * 16)
 
 
 def kernel(
@@ -365,7 +365,7 @@
 
     units = 2 * heads
     matched = n == heads
-    ahead = 6
+    ahead = 4
     begun = units - ahead if matched else 0
 
     def head_at(i):

time: 107 us -> 105 us (0.981)
  Pallas kernels: 102 us -> 99.6 us
    pallas_call x1, Pallas kernels: 102 us -> 99.6 us  [body(): pl.pallas_call(functools.partial(kernel, n, heads), out_shape=(jax.ShapeD...]
where the time goes in v4:
time: 105 us; the launch traced here: 104 us
  Pallas kernels  99.6 us (95%)
  local copies, waits for them, and re-layouts  4.01 us (4%)
    pallas_call x1, Pallas kernels, body(): pl.pallas_call(functools.partial(kernel, n, heads), out_shape=(jax.ShapeD...  99.6 us
    unnamed x4, local copies, waits for them, and re-layouts  4.01 us

profile of v4, /device:TPU:0, one launch (start us, length us, event | category | flops | bytes accessed | tf_op | source)
XLA Modules:
  0.0 104.3 jit_solution(13315055378097099953)
XLA Ops:
  0.6 99.6 %shard_map.113 = (bf16[2,256,2048]{2,1,0:T(8,128)(2,1)}, f32[64,2048]{1,0:T(8,128)}) custom-call(s32[1,4]{1,0:T(1,128)} %order_ref.1, s32[32]{0:T(128)} %counts_ref.1, f32[1,2048]{1,0:T(1,128)} %bitcast.4, bf16[2,256,2048]{2,1,0:T(8,128)(2,1)} %tok_ref.1, bf16[16,256]{1,0:T(8,128)(2,1)} %bitcast.5, bf16[256,1024]{1,0:T(8,128)(2,1)} %wq_ref.1, ...), custom_call_target="tpu_custom_call" | custom-call | tf_op jit(solution)/shard_map/pallas_call | solution.py:442
  100.3 0.0 copy-start
  100.3 3.2 %copy.14 = bf16[2,256,2048]{2,1,0:T(8,128)(2,1)} copy(bf16[2,256,2048]{2,1,0:T(8,128)(2,1)} %get-tuple-element.4) | data formatting | bytes 4194304
  103.5 0.0 copy-done
  103.5 0.8 copy.15
Async XLA Ops:
  100.3 3.2 %copy-start = (f32[64,2048]{1,0:T(8,128)S(1)}, f32[64,2048]{1,0:T(8,128)}, u32[]{:S(2)}) copy-start(f32[64,2048]{1,0:T(8,128)} %get-tuple-element.5) | copy-start | bytes 1572868
